TPU v7x, 256 devices: a whole 4x4x8 slice. The times are simulated.
256 devices in a mesh: dp: 4 (over z_hi), ctx: 64 (over z_lo, x, y, core).
Axes of the slice: x: 4, y: 4, z: 8 (z_hi: 4, z_lo: 2; z = z_hi * 2 + z_lo), core: 2. Of those that a mesh axis runs over, the one named last changes fastest.
Arguments:
- query_proj: bfloat16 [1024, 32768], P(None, ('dp', 'ctx')), may hold values from -6 to 6
- key_proj: bfloat16 [1024, 32768], P(None, ('dp', 'ctx')), may hold values from -6 to 6
- value_proj: bfloat16 [1024, 32768], P(None, ('dp', 'ctx')), may hold values from -6 to 6
- filter_taps: bfloat16 [1024, 32768], P(None, ('dp', 'ctx')), may hold values from -1.1 to 1.1
- grad_out: bfloat16 [1024, 32768], P(None, ('dp', 'ctx')), may hold values from -1.5 to 1.5
Outputs:
- grad_query: bfloat16 [1024, 32768], P(None, ('dp', 'ctx'))
- grad_key: bfloat16 [1024, 32768], P(None, ('dp', 'ctx'))
- grad_value: bfloat16 [1024, 32768], P(None, ('dp', 'ctx'))
- grad_filter: bfloat16 [1024, 32768], P(None, ('dp', 'ctx'))
All inputs are finite; a program needn't handle non-finite values.
Results may differ from a plain program's by a relative error of at most 0.0058.
Values may be sent and summed in bfloat16 or wider, within the bound.
A program may use at most 64 MiB of HBM per device.

v0:
```python
import functools

import jax
import jax.numpy as jnp
import numpy as np
from jax import lax
from jax.experimental import pallas as pl
from jax.experimental.pallas import tpu as pltpu
from jax.sharding import PartitionSpec as P

MESH = pl.DeviceIdType.MESH
DEVICES = 256
INNER = 64
SIDE = 16
TOKENS = 128
CHANNELS = 1024
PARTS = 2
HELD = CHANNELS // DEVICES // PARTS
ROWS = 3 * HELD * DEVICES
SLAB = CHANNELS // PARTS
BF16 = jnp.bfloat16
F32 = jnp.float32


def make_tables():
    length = DEVICES * TOKENS
    outer = np.arange(DEVICES)
    inner = np.arange(TOKENS)
    theta = 2.0 * np.pi * (outer[:, None] + 0.25) * outer[None, :] / DEVICES
    first = np.concatenate([np.cos(theta), -np.sin(theta)], axis=0)
    last = first.T / length
    phase = 2.0 * np.pi * (outer[:, None] + 0.25) * inner[None, :] / length
    twist = np.concatenate([np.cos(phase), -np.sin(phase)], axis=1)
    turn = 2.0 * np.pi * ((inner[:, None] * inner[None, :]) % TOKENS) / TOKENS
    cosine, sine = np.cos(turn), np.sin(turn)
    there = np.block([[cosine, -sine], [sine, cosine]])
    back = np.block([[cosine, sine], [-sine, cosine]])
    return tuple(table.astype(np.float32) for table in (first, there, back, last, twist))


def where(device):
    return (device // INNER, device % INNER)


def at_offset(me, step):
    z = (me // 32 + step) % 8
    x = (me // 8 + step // 64) % 4
    y = (me // 2 + step // 16) % 4
    core = (me + step // 8) % 2
    return z * 32 + x * 8 + y * 2 + core


def one_dot(left, right):
    return jnp.dot(left, right, preferred_element_type=F32)


def halves(value):
    high = value.astype(BF16)
    return high, (value - high.astype(F32)).astype(BF16)


def kernel(
    query_hbm, key_hbm, value_hbm, taps_hbm, grad_hbm, first_hbm, there_hbm, back_hbm, last_hbm, twist_hbm,
    grad_query, grad_key, grad_value, grad_filter,
    query, key, value, taps, grad, first_wide, there_wide, back_wide, last_wide, twist, first, there, back, last,
    sent, landed, rows, result, returned, returned_in, load_sem, send_sem, recv_sem, return_sem, back_sem, cross_sem,
):
    me = lax.axis_index("dp") * INNER + lax.axis_index("ctx")
    barrier = pltpu.get_barrier_semaphore()
    group, member = me // SIDE, me % SIDE

    def along(step):
        return where(group * SIDE + (member + step) % SIDE)

    def across(step):
        return where(((group + step) % SIDE) * SIDE + member)

    @pl.loop(1, SIDE)
    def _(step):
        pl.semaphore_signal(barrier, inc=1, device_id=along(step), device_id_type=MESH)
        pl.semaphore_signal(barrier, inc=1, device_id=across(step), device_id_type=MESH)

    loads = []
    for place, (source, target) in enumerate((
        (key_hbm, key), (value_hbm, value), (grad_hbm, grad), (query_hbm, query), (taps_hbm, taps),
        (first_hbm, first_wide), (there_hbm, there_wide), (back_hbm, back_wide), (last_hbm, last_wide), (twist_hbm, twist),
    )):
        copy = pltpu.make_async_copy(source, target, load_sem.at[place])
        copy.start()
        loads.append(copy)
    for copy in loads[:5]:
        copy.wait()

    for part in range(PARTS):
        lines = pl.ds(part * SLAB, SLAB)
        source = key[lines].astype(F32) * value[lines].astype(F32)
        signal = grad[lines].astype(F32) * query[lines].astype(F32)
        sent[part, :, 0] = taps[lines].astype(F32).reshape(DEVICES, HELD, TOKENS).astype(BF16)
        sent[part, :, 1] = source.reshape(DEVICES, HELD, TOKENS).astype(BF16)
        sent[part, :, 2] = signal.reshape(DEVICES, HELD, TOKENS).astype(BF16)

    for copy in loads[5:]:
        copy.wait()
    for wide, table in ((first_wide, first), (there_wide, there), (back_wide, back), (last_wide, last)):
        table[0], table[1] = halves(wide[...])

    pl.semaphore_wait(barrier, 2 * (SIDE - 1))

    @pl.loop(1, SIDE)
    def _(step):
        pl.semaphore_signal(cross_sem, inc=1, device_id=across(step), device_id_type=MESH)

    pl.semaphore_wait(cross_sem, SIDE - 1)

    def scatter(outgoing, incoming, part, out_sem, in_sem):
        @pl.loop(1, DEVICES, unroll=5)
        def _(step):
            device = at_offset(me, step)
            pltpu.make_async_remote_copy(
                src_ref=outgoing.at[part, device],
                dst_ref=incoming.at[part, me],
                send_sem=out_sem.at[part],
                recv_sem=in_sem.at[part],
                device_id=where(device),
                device_id_type=MESH,
            ).start()

        pltpu.make_async_copy(outgoing.at[part, me], incoming.at[part, me], in_sem.at[part]).start()

    def all_in(incoming, part, in_sem):
        pltpu.make_async_copy(incoming.at[part], incoming.at[part], in_sem.at[part]).wait()

    def all_out(outgoing, part, out_sem):
        span = outgoing.at[part, pl.ds(0, DEVICES - 1)]
        pltpu.make_async_copy(span, span, out_sem.at[part]).wait()

    for part in range(PARTS):
        scatter(sent, landed, part, send_sem, recv_sem)

    def twisted(real, imag, sign):
        turn_real, turn_imag = twist[:, :TOKENS], sign * twist[:, TOKENS:]
        return real * turn_real - imag * turn_imag, real * turn_imag + imag * turn_real

    def triple(value, table):
        high, low = halves(value)
        return one_dot(high, table[0]) + (one_dot(low, table[0]) + one_dot(high, table[1]))

    @pl.loop(0, PARTS)
    def _(part):
        all_in(landed, part, recv_sem)
        rows[...] = landed[part].astype(F32).reshape(ROWS, TOKENS)
        columns = jnp.concatenate(
            [rows[pl.ds(line, DEVICES, stride=3 * HELD), :].astype(BF16) for line in range(3 * HELD)], axis=1
        )
        stage = one_dot(first[0], columns) + one_dot(first[1], columns)
        freq = []
        for line in range(3 * HELD):
            lanes = slice(line * TOKENS, (line + 1) * TOKENS)
            real, imag = twisted(stage[:DEVICES, lanes], stage[DEVICES:, lanes], 1.0)
            spectrum = triple(jnp.concatenate([real, imag], axis=1), there)
            freq.append((spectrum[:, :TOKENS], spectrum[:, TOKENS:]))
        pieces = []
        for which in range(3):
            for held in range(HELD):
                taps_freq, source_freq, signal_freq = (freq[array * HELD + held] for array in range(3))
                one, two = ((taps_freq, source_freq), (taps_freq, signal_freq), (source_freq, signal_freq))[which]
                if which == 0:
                    real = one[0] * two[0] - one[1] * two[1]
                    imag = one[0] * two[1] + one[1] * two[0]
                else:
                    real = one[0] * two[0] + one[1] * two[1]
                    imag = one[0] * two[1] - one[1] * two[0]
                spread = triple(jnp.concatenate([real, imag], axis=1), back)
                real, imag = twisted(spread[:, :TOKENS], spread[:, TOKENS:], -1.0)
                pieces.append(jnp.concatenate([real, imag], axis=0))
        high, low = halves(jnp.concatenate(pieces, axis=1))
        final = one_dot(last[0], high) + (one_dot(last[0], low) + one_dot(last[1], high))
        for line in range(3 * HELD):
            result[pl.ds(line, DEVICES, stride=3 * HELD), :] = final[:, line * TOKENS:(line + 1) * TOKENS]
        returned[part] = result[...].reshape(DEVICES, 3, HELD, TOKENS).astype(BF16)
        scatter(returned, returned_in, part, return_sem, back_sem)

    for part in range(PARTS):
        all_in(returned_in, part, back_sem)
        lines = pl.ds(part * SLAB, SLAB)
        convolved = returned_in[part, :, 0].astype(F32).reshape(SLAB, TOKENS)
        back_signal = returned_in[part, :, 1].astype(F32).reshape(SLAB, TOKENS)
        grad_query[lines] = (grad[lines].astype(F32) * convolved).astype(BF16)
        grad_key[lines] = (back_signal * value[lines].astype(F32)).astype(BF16)
        grad_value[lines] = (back_signal * key[lines].astype(F32)).astype(BF16)
        grad_filter[lines] = returned_in[part, :, 2].astype(F32).reshape(SLAB, TOKENS).astype(BF16)
    for part in range(PARTS):
        all_out(sent, part, send_sem)
        all_out(returned, part, return_sem)


def on_device(query_proj, key_proj, value_proj, filter_taps, grad_out):
    tables = make_tables()
    block = (CHANNELS, TOKENS)
    packed = (PARTS, DEVICES, 3, HELD, TOKENS)
    return pl.pallas_call(
        kernel,
        out_shape=[jax.ShapeDtypeStruct(block, BF16)] * 4,
        in_specs=[pl.BlockSpec(memory_space=pltpu.HBM)] * 10,
        out_specs=[pl.BlockSpec(memory_space=pltpu.VMEM)] * 4,
        scratch_shapes=[pltpu.VMEM(block, BF16)] * 5
        + [pltpu.VMEM(table.shape, F32) for table in tables]
        + [pltpu.VMEM((2,) + table.shape, BF16) for table in tables[:4]]
        + [
            pltpu.VMEM(packed, BF16),
            pltpu.VMEM(packed, BF16),
            pltpu.VMEM((ROWS, TOKENS), F32),
            pltpu.VMEM((ROWS, TOKENS), F32),
            pltpu.VMEM(packed, BF16),
            pltpu.VMEM(packed, BF16),
            pltpu.SemaphoreType.DMA((10,)),
            pltpu.SemaphoreType.DMA((PARTS,)),
            pltpu.SemaphoreType.DMA((PARTS,)),
            pltpu.SemaphoreType.DMA((PARTS,)),
            pltpu.SemaphoreType.DMA((PARTS,)),
            pltpu.SemaphoreType.REGULAR,
        ],
        compiler_params=pltpu.CompilerParams(
            collective_id=0, has_side_effects=True, vmem_limit_bytes=48 * 2**20
        ),
        name="gated_conv_backward",
    )(query_proj, key_proj, value_proj, filter_taps, grad_out, *(jnp.asarray(table) for table in tables))


def solution(mesh):
    spec = P(None, ("dp", "ctx"))
    return jax.shard_map(on_device, mesh=mesh, in_specs=(spec,) * 5, out_specs=(spec,) * 4, check_vma=False)
```

profile of v0, /device:TPU:1, one launch (start us, length us, event | category | flops | bytes accessed | tf_op | source)
XLA Modules:
  0.0 75.6 jit_solution(2687978407719147763)
XLA Ops:
  0.6 0.0 copy-start
  0.6 1.0 %copy-done = f32[256,512]{1,0:T(8,128)S(1)} copy-done((f32[256,512]{1,0:T(8,128)S(1)}, f32[256,512]{1,0:T(8,128)}, u32[]{:S(2)}) %copy-start) | copy-done | bytes 524312
  1.7 0.0 copy-start.1
  1.7 1.0 %copy-done.1 = f32[512,256]{1,0:T(8,128)S(1)} copy-done((f32[512,256]{1,0:T(8,128)S(1)}, f32[512,256]{1,0:T(8,128)}, u32[]{:S(2)}) %copy-start.1) | copy-done | bytes 524312
  2.7 0.0 copy-start.2
  2.7 0.9 %copy-done.2 = bf16[1024,128]{1,0:T(8,128)(2,1)S(1)} copy-done((bf16[1024,128]{1,0:T(8,128)(2,1)S(1)}, bf16[1024,128]{1,0:T(8,128)(2,1)}, u32[]{:S(2)}) %copy-start.2) | copy-done | bytes 262168
  3.7 0.0 copy-start.3
  3.7 0.9 %copy-done.3 = bf16[1024,128]{1,0:T(8,128)(2,1)S(1)} copy-done((bf16[1024,128]{1,0:T(8,128)(2,1)S(1)}, bf16[1024,128]{1,0:T(8,128)(2,1)}, u32[]{:S(2)}) %copy-start.3) | copy-done | bytes 262168
  4.6 0.0 copy-start.4
  4.6 0.9 %copy-done.4 = bf16[1024,128]{1,0:T(8,128)(2,1)S(1)} copy-done((bf16[1024,128]{1,0:T(8,128)(2,1)S(1)}, bf16[1024,128]{1,0:T(8,128)(2,1)}, u32[]{:S(2)}) %copy-start.4) | copy-done | bytes 262168
  5.6 0.0 copy-start.5
  5.6 0.9 %copy-done.5 = bf16[1024,128]{1,0:T(8,128)(2,1)S(1)} copy-done((bf16[1024,128]{1,0:T(8,128)(2,1)S(1)}, bf16[1024,128]{1,0:T(8,128)(2,1)}, u32[]{:S(2)}) %copy-start.5) | copy-done | bytes 262168
  6.5 0.0 copy-start.6
  6.5 0.9 %copy-done.6 = bf16[1024,128]{1,0:T(8,128)(2,1)S(1)} copy-done((bf16[1024,128]{1,0:T(8,128)(2,1)S(1)}, bf16[1024,128]{1,0:T(8,128)(2,1)}, u32[]{:S(2)}) %copy-start.6) | copy-done | bytes 262168
  7.5 0.0 copy-start.7
  7.5 0.9 %copy-done.7 = f32[256,256]{1,0:T(8,128)S(1)} copy-done((f32[256,256]{1,0:T(8,128)S(1)}, f32[256,256]{1,0:T(8,128)}, u32[]{:S(2)}) %copy-start.7) | copy-done | bytes 262168
  8.4 0.0 copy-start.8
  8.4 0.9 %copy-done.8 = f32[256,256]{1,0:T(8,128)S(1)} copy-done((f32[256,256]{1,0:T(8,128)S(1)}, f32[256,256]{1,0:T(8,128)}, u32[]{:S(2)}) %copy-start.8) | copy-done | bytes 262168
  9.4 0.9 %copy-done.9 = f32[256,256]{1,0:T(8,128)S(1)} copy-done((f32[256,256]{1,0:T(8,128)S(1)}, f32[256,256]{1,0:T(8,128)}, u32[]{:S(2)}) %copy-start.9) | copy-done | bytes 262168
  10.3 62.4 %gated_conv_backward.1 = (bf16[1024,128]{1,0:T(8,128)(2,1)S(1)}, bf16[1024,128]{1,0:T(8,128)(2,1)S(1)}, bf16[1024,128]{1,0:T(8,128)(2,1)S(1)}, bf16[1024,128]{1,0:T(8,128)(2,1)S(1)}) custom-call(bf16[1024,128]{1,0:T(8,128)(2,1)S(1)} %copy-done.2, bf16[1024,128]{1,0:T(8,128)(2,1)S(1)} %copy-done.3, bf16[1024,128]{1,0:T(8,128)(2,1)S(1)} %copy-done.4, ...), custom_call_target="tpu_custom_call" | custom-call | tf_op jit(solution)/shard_map/gated_conv_backward/pallas_call | solution.py:201
  72.8 0.7 copy.18
  73.5 0.7 copy.19
  74.2 0.7 copy.20
  74.9 0.7 copy.21
  (1 shorter events, 0.0 us)
Async XLA Ops:
  0.6 1.0 %copy-start = (f32[256,512]{1,0:T(8,128)S(1)}, f32[256,512]{1,0:T(8,128)}, u32[]{:S(2)}) copy-start(f32[256,512]{1,0:T(8,128)} %constant.13.clone.last_hbm) | copy-start | bytes 1572868
  1.7 1.0 %copy-start.1 = (f32[512,256]{1,0:T(8,128)S(1)}, f32[512,256]{1,0:T(8,128)}, u32[]{:S(2)}) copy-start(f32[512,256]{1,0:T(8,128)} %constant.10.clone.first_hbm) | copy-start | bytes 1572868
  2.7 0.9 %copy-start.2 = (bf16[1024,128]{1,0:T(8,128)(2,1)S(1)}, bf16[1024,128]{1,0:T(8,128)(2,1)}, u32[]{:S(2)}) copy-start(bf16[1024,128]{1,0:T(8,128)(2,1)} %query_hbm.1) | copy-start | bytes 786436
  3.7 0.9 %copy-start.3 = (bf16[1024,128]{1,0:T(8,128)(2,1)S(1)}, bf16[1024,128]{1,0:T(8,128)(2,1)}, u32[]{:S(2)}) copy-start(bf16[1024,128]{1,0:T(8,128)(2,1)} %key_hbm.1) | copy-start | bytes 786436
  4.6 0.9 %copy-start.4 = (bf16[1024,128]{1,0:T(8,128)(2,1)S(1)}, bf16[1024,128]{1,0:T(8,128)(2,1)}, u32[]{:S(2)}) copy-start(bf16[1024,128]{1,0:T(8,128)(2,1)} %value_hbm.1) | copy-start | bytes 786436
  5.6 0.9 %copy-start.5 = (bf16[1024,128]{1,0:T(8,128)(2,1)S(1)}, bf16[1024,128]{1,0:T(8,128)(2,1)}, u32[]{:S(2)}) copy-start(bf16[1024,128]{1,0:T(8,128)(2,1)} %taps_hbm.1) | copy-start | bytes 786436
  6.5 0.9 %copy-start.6 = (bf16[1024,128]{1,0:T(8,128)(2,1)S(1)}, bf16[1024,128]{1,0:T(8,128)(2,1)}, u32[]{:S(2)}) copy-start(bf16[1024,128]{1,0:T(8,128)(2,1)} %grad_hbm.1) | copy-start | bytes 786436
  7.5 0.9 %copy-start.7 = (f32[256,256]{1,0:T(8,128)S(1)}, f32[256,256]{1,0:T(8,128)}, u32[]{:S(2)}) copy-start(f32[256,256]{1,0:T(8,128)} %constant.14.clone.twist_hbm) | copy-start | bytes 786436
  8.4 0.9 %copy-start.8 = (f32[256,256]{1,0:T(8,128)S(1)}, f32[256,256]{1,0:T(8,128)}, u32[]{:S(2)}) copy-start(f32[256,256]{1,0:T(8,128)} %constant.12.clone.back_hbm) | copy-start | bytes 786436
  9.4 0.9 %copy-start.9 = (f32[256,256]{1,0:T(8,128)S(1)}, f32[256,256]{1,0:T(8,128)}, u32[]{:S(2)}) copy-start(f32[256,256]{1,0:T(8,128)} %constant.11.clone.there_hbm) | copy-start | bytes 786436
where the time goes:
time: 76 us; the launch traced here: 75.6 us
  Pallas kernels  62.4 us (82%)
  local copies, waits for them, and re-layouts  12.5 us (16%)
    pallas_call x1, Pallas kernels, on_device(): pl.pallas_call(kernel, out_shape=[jax.ShapeDtypeStruct(block, BF16)] * 4,...  62.4 us
    unnamed x24, local copies, waits for them, and re-layouts  12.5 us

commit v1 on v0

v1 whole, which is shorter than its diff:
```python
import jax
import jax.numpy as jnp
import numpy as np
from jax import lax
from jax.experimental import pallas as pl
from jax.experimental.pallas import tpu as pltpu
from jax.sharding import PartitionSpec as P

LOGICAL = pl.DeviceIdType.LOGICAL
DEVICES = 256
INNER = 64
TOKENS = 128
CHANNELS = 1024
PARTS = 2
HELD = CHANNELS // DEVICES // PARTS
LINES = 3 * HELD
ROWS = LINES * DEVICES
SLAB = CHANNELS // PARTS
RING = (4, 3, 5, 2, 6, 1, 7, 0)
BF16 = jnp.bfloat16
F32 = jnp.float32


def make_tables():
    length = DEVICES * TOKENS
    outer = np.arange(DEVICES)
    inner = np.arange(TOKENS)
    theta = 2.0 * np.pi * (outer[:, None] + 0.25) * outer[None, :] / DEVICES
    cosine, sine = np.cos(theta), -np.sin(theta)
    phase = 2.0 * np.pi * (outer[:, None] + 0.25) * inner[None, :] / length
    twist = np.concatenate([np.cos(phase), -np.sin(phase)], axis=1)
    turn = 2.0 * np.pi * ((inner[:, None] * inner[None, :]) % TOKENS) / TOKENS
    there = np.block([[np.cos(turn), -np.sin(turn)], [np.sin(turn), np.cos(turn)]])
    back = np.block([[np.cos(turn), np.sin(turn)], [-np.sin(turn), np.cos(turn)]])
    stacked = [cosine, sine, there, back, cosine.T / length, sine.T / length, twist]
    return np.concatenate(stacked, axis=0).astype(np.float32)


def one_dot(left, right):
    return jnp.dot(left, right, preferred_element_type=F32)


def halves(value):
    high = value.astype(BF16)
    return high, (value - high.astype(F32)).astype(BF16)


def kernel(
    query_hbm, key_hbm, value_hbm, taps_hbm, grad_hbm, table_hbm, out,
    query, key, value, taps, grad, table, split, sent, landed, rows, result, returned, returned_in,
    load_sem, send_sem, recv_sem, return_sem, back_sem, cross_sem,
):
    me = lax.axis_index("dp") * INNER + lax.axis_index("ctx")
    low = lax.rem(me, 32)
    column = low // 8
    row = lax.rem(low // 2, 4)
    core = lax.rem(low, 2)
    ring = [lax.rem(me // 32 + step, 8) * 32 for step in range(8)]

    def beside(step_x, step_y, step_core):
        return lax.rem(column + step_x, 4) * 8 + lax.rem(row + step_y, 4) * 2 + lax.rem(core + step_core, 2)

    barrier = pltpu.get_barrier_semaphore()

    def greet(semaphore, device):
        pl.semaphore_signal(semaphore, inc=1, device_id=device, device_id_type=LOGICAL)

    for step in range(1, 4):
        greet(barrier, ring[0] + beside(0, step, 0))
    for step in RING[:7]:
        greet(barrier, ring[step] + low)

    @pl.loop(1, 8)
    def _(pair):
        place = beside(pair // 2, 0, lax.rem(pair, 2))
        for step in RING:
            greet(barrier, ring[step] + place)

    loads = []
    for place, (source, target) in enumerate((
        (key_hbm, key), (value_hbm, value), (grad_hbm, grad), (query_hbm, query), (taps_hbm, taps), (table_hbm, table),
    )):
        copy = pltpu.make_async_copy(source, target, load_sem.at[place])
        copy.start()
        loads.append(copy)
    for copy in loads[:5]:
        copy.wait()

    def pack(part):
        lines = pl.ds(part * SLAB, SLAB)
        shape = (DEVICES, HELD, TOKENS)
        sent[part, :, 0] = taps[lines].astype(F32).reshape(shape).astype(BF16)
        sent[part, :, 1] = (key[lines].astype(F32) * value[lines].astype(F32)).reshape(shape).astype(BF16)
        sent[part, :, 2] = (grad[lines].astype(F32) * query[lines].astype(F32)).reshape(shape).astype(BF16)

    def scatter(outgoing, incoming, part, out_sem, in_sem, wait=None):
        def send(device):
            pltpu.make_async_remote_copy(
                src_ref=outgoing.at[part, device],
                dst_ref=incoming.at[part, me],
                send_sem=out_sem.at[part],
                recv_sem=in_sem.at[part],
                device_id=device,
                device_id_type=LOGICAL,
            ).start()

        pltpu.make_async_copy(outgoing.at[part, me], incoming.at[part, me], in_sem.at[part]).start()
        for step in RING[:7]:
            send(ring[step] + low)

        def rest(step_y, first):
            @pl.loop(first, 8)
            def _(pair):
                place = beside(pair // 2, step_y, lax.rem(pair, 2))
                for step in RING:
                    send(ring[step] + place)

        for step_y in range(4):
            if wait is not None and step_y:
                wait(step_y)
            rest(step_y, 0 if step_y else 1)

    def all_in(incoming, part, in_sem):
        pltpu.make_async_copy(incoming.at[part], incoming.at[part], in_sem.at[part]).wait()

    def all_out(outgoing, part, out_sem):
        span = outgoing.at[part, pl.ds(0, DEVICES - 1)]
        pltpu.make_async_copy(span, span, out_sem.at[part]).wait()

    pack(0)
    pl.semaphore_wait(barrier, 66)
    for step in range(1, 4):
        greet(cross_sem.at[step], ring[0] + beside(0, step, 0))
    scatter(sent, landed, 0, send_sem, recv_sem, lambda step: pl.semaphore_wait(cross_sem.at[4 - step], 1))
    pack(1)
    scatter(sent, landed, 1, send_sem, recv_sem)

    loads[5].wait()
    split[0], split[1] = halves(table[pl.ds(0, 1536)])

    def twisted(real, imag, sign):
        turn_real, turn_imag = table[pl.ds(1536, DEVICES), :TOKENS], sign * table[pl.ds(1536, DEVICES), TOKENS:]
        return real * turn_real - imag * turn_imag, real * turn_imag + imag * turn_real

    def triple(value, lines):
        high, below = halves(value)
        return one_dot(high, split[0, lines]) + (one_dot(below, split[0, lines]) + one_dot(high, split[1, lines]))

    @pl.loop(0, PARTS)
    def _(part):
        all_in(landed, part, recv_sem)
        rows[...] = landed[part].astype(F32).reshape(ROWS, TOKENS)
        columns = jnp.concatenate(
            [rows[pl.ds(line, DEVICES, stride=LINES), :].astype(BF16) for line in range(LINES)], axis=1
        )
        stage = one_dot(split[0, 0:512], columns) + one_dot(split[1, 0:512], columns)
        freq = []
        for line in range(LINES):
            lanes = slice(line * TOKENS, (line + 1) * TOKENS)
            real, imag = twisted(stage[:DEVICES, lanes], stage[DEVICES:, lanes], 1.0)
            spectrum = triple(jnp.concatenate([real, imag], axis=1), slice(512, 768))
            freq.append((spectrum[:, :TOKENS], spectrum[:, TOKENS:]))
        pieces = []
        for which in range(3):
            for held in range(HELD):
                taps_freq, source_freq, signal_freq = (freq[array * HELD + held] for array in range(3))
                one, two = ((taps_freq, source_freq), (taps_freq, signal_freq), (source_freq, signal_freq))[which]
                if which == 0:
                    real = one[0] * two[0] - one[1] * two[1]
                    imag = one[0] * two[1] + one[1] * two[0]
                else:
                    real = one[0] * two[0] + one[1] * two[1]
                    imag = one[0] * two[1] - one[1] * two[0]
                spread = triple(jnp.concatenate([real, imag], axis=1), slice(768, 1024))
                pieces.append(twisted(spread[:, :TOKENS], spread[:, TOKENS:], -1.0))
        final = 0.0
        for side in range(2):
            high, below = halves(jnp.concatenate([piece[side] for piece in pieces], axis=1))
            lines = slice(1024 + side * DEVICES, 1280 + side * DEVICES)
            final += one_dot(split[0, lines], high) + (one_dot(split[0, lines], below) + one_dot(split[1, lines], high))
        for line in range(LINES):
            result[pl.ds(line, DEVICES, stride=LINES), :] = final[:, line * TOKENS:(line + 1) * TOKENS]
        returned[part] = result[...].reshape(DEVICES, 3, HELD, TOKENS).astype(BF16)
        scatter(returned, returned_in, part, return_sem, back_sem)

    for part in range(PARTS):
        all_in(returned_in, part, back_sem)
        for which in range(3):
            out[which, pl.ds(part * SLAB, SLAB)] = returned_in[part, :, which].astype(F32).reshape(SLAB, TOKENS).astype(BF16)
    for part in range(PARTS):
        all_out(sent, part, send_sem)
        all_out(returned, part, return_sem)


def gate(back, key, value, grad, grad_query, grad_key, grad_value, grad_filter):
    back_signal = back[1].astype(F32)
    grad_query[...] = (grad[...].astype(F32) * back[0].astype(F32)).astype(BF16)
    grad_key[...] = (back_signal * value[...].astype(F32)).astype(BF16)
    grad_value[...] = (back_signal * key[...].astype(F32)).astype(BF16)
    grad_filter[...] = back[2]


def on_device(query_proj, key_proj, value_proj, filter_taps, grad_out):
    table = make_tables()
    block = (CHANNELS, TOKENS)
    packed = (PARTS, DEVICES, 3, HELD, TOKENS)
    back = pl.pallas_call(
        kernel,
        out_shape=jax.ShapeDtypeStruct((3,) + block, BF16),
        in_specs=[pl.BlockSpec(memory_space=pltpu.HBM)] * 6,
        out_specs=pl.BlockSpec(memory_space=pltpu.VMEM),
        scratch_shapes=[pltpu.VMEM(block, BF16)] * 5
        + [
            pltpu.VMEM(table.shape, F32),
            pltpu.VMEM((2, 1536, DEVICES), BF16),
            pltpu.VMEM(packed, BF16),
            pltpu.VMEM(packed, BF16),
            pltpu.VMEM((ROWS, TOKENS), F32),
            pltpu.VMEM((ROWS, TOKENS), F32),
            pltpu.VMEM(packed, BF16),
            pltpu.VMEM(packed, BF16),
            pltpu.SemaphoreType.DMA((6,)),
            pltpu.SemaphoreType.DMA((PARTS,)),
            pltpu.SemaphoreType.DMA((PARTS,)),
            pltpu.SemaphoreType.DMA((PARTS,)),
            pltpu.SemaphoreType.DMA((PARTS,)),
            pltpu.SemaphoreType.REGULAR((4,)),
        ],
        compiler_params=pltpu.CompilerParams(
            collective_id=0, has_side_effects=True, vmem_limit_bytes=63 * 2**20
        ),
        name="transform_and_exchange",
    )(query_proj, key_proj, value_proj, filter_taps, grad_out, jnp.asarray(table))
    return pl.pallas_call(
        gate,
        grid=(2,),
        out_shape=[jax.ShapeDtypeStruct(block, BF16)] * 4,
        in_specs=[pl.BlockSpec((3, CHANNELS // 2, TOKENS), lambda i: (0, i, 0))]
        + [pl.BlockSpec((CHANNELS // 2, TOKENS), lambda i: (i, 0))] * 3,
        out_specs=[pl.BlockSpec((CHANNELS // 2, TOKENS), lambda i: (i, 0))] * 4,
        name="gate_results",
    )(back, key_proj, value_proj, grad_out)


def solution(mesh):
    spec = P(None, ("dp", "ctx"))
    return jax.shard_map(on_device, mesh=mesh, in_specs=(spec,) * 5, out_specs=(spec,) * 4, check_vma=False)
```

time: 76 us -> 56.1 us (0.74)
  local copies, waits for them, and re-layouts: 12.5 us -> 0 us
  Pallas kernels: 62.4 us -> 55.4 us
    unnamed x24 -> x0, local copies, waits for them, and re-layouts: 12.5 us -> none
    pallas_call x1 -> x2, Pallas kernels: 62.4 us -> 55.4 us  [the longest x1 53.1 us: on_device(): pl.pallas_call(kernel, out_shape=jax.ShapeDtypeStruct((3,) + block, BF16)...]
where the time goes in v1:
time: 56.1 us; the launch traced here: 56 us
  Pallas kernels  55.4 us (99%)
  between operations  0.64 us (1%)
    pallas_call x1, Pallas kernels, on_device(): pl.pallas_call(kernel, out_shape=jax.ShapeDtypeStruct((3,) + block, BF16)...  53.1 us
    pallas_call x1, Pallas kernels, on_device(): pl.pallas_call(gate, grid=(2,), out_shape=[jax.ShapeDtypeStruct(block, BF...  2.22 us

profile of v1, /device:TPU:1, one launch (start us, length us, event | category | flops | bytes accessed | tf_op | source)
XLA Modules:
  0.0 56.0 jit_solution(4405988039663031933)
XLA Ops:
  0.6 53.1 %transform_and_exchange.1.back = bf16[3,1024,128]{2,1,0:T(8,128)(2,1)} custom-call(bf16[1024,128]{1,0:T(8,128)(2,1)} %query_hbm.1, bf16[1024,128]{1,0:T(8,128)(2,1)} %key.1, bf16[1024,128]{1,0:T(8,128)(2,1)} %value.1, bf16[1024,128]{1,0:T(8,128)(2,1)} %taps_hbm.1, bf16[1024,128]{1,0:T(8,128)(2,1)} %grad.1, f32[1792,256]{1,0:T(8,128)} %constant.2.clone.table_hbm), custom_call_target="tpu_custom_call" | custom-call | tf_op jit(solution)/shard_map/transform_and_exchange/pallas_call | solution.py:207
  53.8 2.2 %gate_results.1 = (bf16[1024,128]{1,0:T(8,128)(2,1)}, bf16[1024,128]{1,0:T(8,128)(2,1)}, bf16[1024,128]{1,0:T(8,128)(2,1)}, bf16[1024,128]{1,0:T(8,128)(2,1)}) custom-call(bf16[3,1024,128]{2,1,0:T(8,128)(2,1)} %transform_and_exchange.1.back, bf16[1024,128]{1,0:T(8,128)(2,1)} %key.1, bf16[1024,128]{1,0:T(8,128)(2,1)} %value.1, bf16[1024,128]{1,0:T(8,128)(2,1)} %grad.1), custom_call_target="tpu_custom_call" | custom-call | tf_op jit(solution)/shard_map/gate_results/pallas_call | solution.py:234

commit v2 on v1

--- a/solution.py
+++ b/solution.py
@@ -66,34 +66,38 @@
         pl.semaphore_signal(semaphore, inc=1, device_id=device, device_id_type=LOGICAL)
 
     for step in range(1, 4):
+        greet(barrier, ring[0] + beside(step, 0, 0))
         greet(barrier, ring[0] + beside(0, step, 0))
-    for step in RING[:7]:
-        greet(barrier, ring[step] + low)
-
-    @pl.loop(1, 8)
-    def _(pair):
-        place = beside(pair // 2, 0, lax.rem(pair, 2))
-        for step in RING:
-            greet(barrier, ring[step] + place)
+    twin = beside(0, 0, 1)
+    for step in RING:
+        if step:
+            greet(barrier, ring[step] + low)
+        greet(barrier, ring[step] + twin)
 
     loads = []
-    for place, (source, target) in enumerate((
-        (key_hbm, key), (value_hbm, value), (grad_hbm, grad), (query_hbm, query), (taps_hbm, taps), (table_hbm, table),
-    )):
-        copy = pltpu.make_async_copy(source, target, load_sem.at[place])
-        copy.start()
-        loads.append(copy)
-    for copy in loads[:5]:
-        copy.wait()
+    for part in range(PARTS):
+        lines = pl.ds(part * SLAB, SLAB)
+        group = []
+        for place, (source, target) in enumerate((
+            (taps_hbm, taps), (key_hbm, key), (value_hbm, value), (grad_hbm, grad), (query_hbm, query),
+        )):
+            copy = pltpu.make_async_copy(source.at[lines], target.at[lines], load_sem.at[part, place])
+            copy.start()
+            group.append(copy)
+        loads.append(group)
+    table_load = pltpu.make_async_copy(table_hbm, table, load_sem.at[0, 5])
+    table_load.start()
 
     def pack(part):
+        for copy in loads[part]:
+            copy.wait()
         lines = pl.ds(part * SLAB, SLAB)
         shape = (DEVICES, HELD, TOKENS)
         sent[part, :, 0] = taps[lines].astype(F32).reshape(shape).astype(BF16)
         sent[part, :, 1] = (key[lines].astype(F32) * value[lines].astype(F32)).reshape(shape).astype(BF16)
         sent[part, :, 2] = (grad[lines].astype(F32) * query[lines].astype(F32)).reshape(shape).astype(BF16)
 
-    def scatter(outgoing, incoming, part, out_sem, in_sem, wait=None):
+    def scatter(outgoing, incoming, part, out_sem, in_sem, wait_x=None, wait_y=None):
         def send(device):
             pltpu.make_async_remote_copy(
                 src_ref=outgoing.at[part, device],
@@ -108,17 +112,28 @@
         for step in RING[:7]:
             send(ring[step] + low)
 
-        def rest(step_y, first):
-            @pl.loop(first, 8)
-            def _(pair):
-                place = beside(pair // 2, step_y, lax.rem(pair, 2))
+        def line(step_x, step_y):
+            for step_core in range(2):
+                place = beside(step_x, step_y, step_core)
                 for step in RING:
                     send(ring[step] + place)
 
-        for step_y in range(4):
-            if wait is not None and step_y:
-                wait(step_y)
-            rest(step_y, 0 if step_y else 1)
+        for step in RING:
+            send(ring[step] + twin)
+        if wait_x is not None:
+            wait_x()
+
+        @pl.loop(1, 4)
+        def _(step_x):
+            line(step_x, 0)
+
+        for step_y in range(1, 4):
+            if wait_y is not None:
+                wait_y(step_y)
+
+            @pl.loop(0, 4)
+            def _(step_x):
+                line(step_x, step_y)
 
     def all_in(incoming, part, in_sem):
         pltpu.make_async_copy(incoming.at[part], incoming.at[part], in_sem.at[part]).wait()
@@ -128,14 +143,24 @@
         pltpu.make_async_copy(span, span, out_sem.at[part]).wait()
 
     pack(0)
-    pl.semaphore_wait(barrier, 66)
+    pl.semaphore_wait(barrier, 21)
     for step in range(1, 4):
-        greet(cross_sem.at[step], ring[0] + beside(0, step, 0))
-    scatter(sent, landed, 0, send_sem, recv_sem, lambda step: pl.semaphore_wait(cross_sem.at[4 - step], 1))
+        greet(cross_sem.at[0, step], ring[0] + beside(step, 0, 0))
+
+    def plane_in():
+        for step in range(1, 4):
+            pl.semaphore_wait(cross_sem.at[0, 4 - step], 1)
+        for step in range(1, 4):
+            greet(cross_sem.at[1, step], ring[0] + beside(0, step, 0))
+
+    def other_in(step):
+        pl.semaphore_wait(cross_sem.at[1, 4 - step], 1)
+
+    scatter(sent, landed, 0, send_sem, recv_sem, plane_in, other_in)
     pack(1)
     scatter(sent, landed, 1, send_sem, recv_sem)
 
-    loads[5].wait()
+    table_load.wait()
     split[0], split[1] = halves(table[pl.ds(0, 1536)])
 
     def twisted(real, imag, sign):
@@ -185,28 +210,41 @@
 
     for part in range(PARTS):
         all_in(returned_in, part, back_sem)
-        for which in range(3):
-            out[which, pl.ds(part * SLAB, SLAB)] = returned_in[part, :, which].astype(F32).reshape(SLAB, TOKENS).astype(BF16)
+        lines = pl.ds(part * SLAB, SLAB)
+        convolved, back_signal, taps_grad = (
+            returned_in[part, :, which].astype(F32).reshape(SLAB, TOKENS) for which in range(3)
+        )
+        out[0, lines] = (grad[lines].astype(F32) * convolved).astype(BF16)
+        out[1, lines] = (back_signal * value[lines].astype(F32)).astype(BF16)
+        out[2, lines] = (back_signal * key[lines].astype(F32)).astype(BF16)
+        out[3, lines] = taps_grad.astype(BF16)
     for part in range(PARTS):
         all_out(sent, part, send_sem)
         all_out(returned, part, return_sem)
 
 
-def gate(back, key, value, grad, grad_query, grad_key, grad_value, grad_filter):
-    back_signal = back[1].astype(F32)
-    grad_query[...] = (grad[...].astype(F32) * back[0].astype(F32)).astype(BF16)
-    grad_key[...] = (back_signal * value[...].astype(F32)).astype(BF16)
-    grad_value[...] = (back_signal * key[...].astype(F32)).astype(BF16)
-    grad_filter[...] = back[2]
+def deal(stacked, grad_query, grad_key, grad_value, grad_filter, sems):
+    copies = [
+        pltpu.make_async_copy(stacked.at[place], target, sems.at[place])
+        for place, target in enumerate((grad_query, grad_key, grad_value, grad_filter))
+    ]
+    for copy in copies:
+        copy.start()
+    for copy in copies:
+        copy.wait()
 
 
 def on_device(query_proj, key_proj, value_proj, filter_taps, grad_out):
     table = make_tables()
     block = (CHANNELS, TOKENS)
     packed = (PARTS, DEVICES, 3, HELD, TOKENS)
-    back = pl.pallas_call(
+    operands = [
+        pltpu.with_memory_space_constraint(operand, pltpu.HBM)
+        for operand in (query_proj, key_proj, value_proj, filter_taps, grad_out, jnp.asarray(table))
+    ]
+    stacked = pl.pallas_call(
         kernel,
-        out_shape=jax.ShapeDtypeStruct((3,) + block, BF16),
+        out_shape=pltpu.VMEM((4,) + block, BF16),
         in_specs=[pl.BlockSpec(memory_space=pltpu.HBM)] * 6,
         out_specs=pl.BlockSpec(memory_space=pltpu.VMEM),
         scratch_shapes=[pltpu.VMEM(block, BF16)] * 5
@@ -219,27 +257,26 @@
             pltpu.VMEM((ROWS, TOKENS), F32),
             pltpu.VMEM(packed, BF16),
             pltpu.VMEM(packed, BF16),
-            pltpu.SemaphoreType.DMA((6,)),
-            pltpu.SemaphoreType.DMA((PARTS,)),
-            pltpu.SemaphoreType.DMA((PARTS,)),
-            pltpu.SemaphoreType.DMA((PARTS,)),
-            pltpu.SemaphoreType.DMA((PARTS,)),
-            pltpu.SemaphoreType.REGULAR((4,)),
+            pltpu.SemaphoreType.DMA((PARTS, 6)),
+            pltpu.SemaphoreType.DMA((PARTS,)),
+            pltpu.SemaphoreType.DMA((PARTS,)),
+            pltpu.SemaphoreType.DMA((PARTS,)),
+            pltpu.SemaphoreType.DMA((PARTS,)),
+            pltpu.SemaphoreType.REGULAR((2, 4)),
         ],
         compiler_params=pltpu.CompilerParams(
-            collective_id=0, has_side_effects=True, vmem_limit_bytes=63 * 2**20
+            collective_id=0, has_side_effects=True, vmem_limit_bytes=40 * 2**20
         ),
         name="transform_and_exchange",
-    )(query_proj, key_proj, value_proj, filter_taps, grad_out, jnp.asarray(table))
+    )(*operands)
     return pl.pallas_call(
-        gate,
-        grid=(2,),
+        deal,
         out_shape=[jax.ShapeDtypeStruct(block, BF16)] * 4,
-        in_specs=[pl.BlockSpec((3, CHANNELS // 2, TOKENS), lambda i: (0, i, 0))]
-        + [pl.BlockSpec((CHANNELS // 2, TOKENS), lambda i: (i, 0))] * 3,
-        out_specs=[pl.BlockSpec((CHANNELS // 2, TOKENS), lambda i: (i, 0))] * 4,
+        in_specs=[pl.BlockSpec(memory_space=pltpu.VMEM)],
+        out_specs=[pl.BlockSpec(memory_space=pltpu.HBM)] * 4,
+        scratch_shapes=[pltpu.SemaphoreType.DMA((4,))],
         name="gate_results",
-    )(back, key_proj, value_proj, grad_out)
+    )(pltpu.with_memory_space_constraint(stacked, pltpu.VMEM))
 
 
 def solution(mesh):

time: 56.1 us -> 54.1 us (0.964)
  Pallas kernels: 55.4 us -> 53.3 us
    pallas_call x2, Pallas kernels: 55.4 us -> 53.3 us  [the longest x1 52.3 us: on_device(): pl.pallas_call(kernel, out_shape=pltpu.VMEM((4,) + block, BF16), in_specs...]
where the time goes in v2:
time: 54.1 us; the launch traced here: 54 us
  Pallas kernels  53.3 us (99%)
  between operations  0.64 us (1%)
    pallas_call x1, Pallas kernels, on_device(): pl.pallas_call(kernel, out_shape=pltpu.VMEM((4,) + block, BF16), in_specs...  52.3 us

profile of v2, /device:TPU:1, one launch (start us, length us, event | category | flops | bytes accessed | tf_op | source)
XLA Modules:
  0.0 54.0 jit_solution(17578355615958864385)
XLA Ops:
  0.6 52.3 %transform_and_exchange.1.stacked = bf16[4,1024,128]{2,1,0:T(8,128)(2,1)S(1)} custom-call(bf16[1024,128]{1,0:T(8,128)(2,1)} %query_hbm.1, bf16[1024,128]{1,0:T(8,128)(2,1)} %key_hbm.1, bf16[1024,128]{1,0:T(8,128)(2,1)} %value_hbm.1, bf16[1024,128]{1,0:T(8,128)(2,1)} %taps_hbm.1, bf16[1024,128]{1,0:T(8,128)(2,1)} %grad_hbm.1, f32[1792,256]{1,0:T(8,128)} %constant.2.clone.table_hbm), custom_call_target="tpu_custom_call" | custom-call | tf_op jit(solution)/shard_map/transform_and_exchange/pallas_call | solution.py:245
  53.0 1.0 %gate_results.1 = (bf16[1024,128]{1,0:T(8,128)(2,1)}, bf16[1024,128]{1,0:T(8,128)(2,1)}, bf16[1024,128]{1,0:T(8,128)(2,1)}, bf16[1024,128]{1,0:T(8,128)(2,1)}) custom-call(bf16[4,1024,128]{2,1,0:T(8,128)(2,1)S(1)} %transform_and_exchange.1.stacked), custom_call_target="tpu_custom_call" | custom-call | tf_op jit(solution)/shard_map/gate_results/pallas_call | solution.py:272

commit v3 on v2

--- a/solution.py
+++ b/solution.py
@@ -65,14 +65,15 @@
     def greet(semaphore, device):
         pl.semaphore_signal(semaphore, inc=1, device_id=device, device_id_type=LOGICAL)
 
-    for step in range(1, 4):
-        greet(barrier, ring[0] + beside(step, 0, 0))
-        greet(barrier, ring[0] + beside(0, step, 0))
     twin = beside(0, 0, 1)
     for step in RING:
         if step:
             greet(barrier, ring[step] + low)
         greet(barrier, ring[step] + twin)
+
+    @pl.loop(1, 16, unroll=5)
+    def _(line):
+        greet(barrier, ring[0] + beside(line // 4, lax.rem(line, 4), 0))
 
     loads = []
     for part in range(PARTS):
@@ -97,43 +98,34 @@
         sent[part, :, 1] = (key[lines].astype(F32) * value[lines].astype(F32)).reshape(shape).astype(BF16)
         sent[part, :, 2] = (grad[lines].astype(F32) * query[lines].astype(F32)).reshape(shape).astype(BF16)
 
-    def scatter(outgoing, incoming, part, out_sem, in_sem, wait_x=None, wait_y=None):
-        def send(device):
-            pltpu.make_async_remote_copy(
-                src_ref=outgoing.at[part, device],
-                dst_ref=incoming.at[part, me],
-                send_sem=out_sem.at[part],
-                recv_sem=in_sem.at[part],
-                device_id=device,
-                device_id_type=LOGICAL,
-            ).start()
-
+    def send(outgoing, incoming, part, out_sem, in_sem, device):
+        pltpu.make_async_remote_copy(
+            src_ref=outgoing.at[part, device],
+            dst_ref=incoming.at[part, me],
+            send_sem=out_sem.at[part],
+            recv_sem=in_sem.at[part],
+            device_id=device,
+            device_id_type=LOGICAL,
+        ).start()
+
+    def send_own_line(*route):
+        outgoing, incoming, part, _, in_sem = route
         pltpu.make_async_copy(outgoing.at[part, me], incoming.at[part, me], in_sem.at[part]).start()
-        for step in RING[:7]:
-            send(ring[step] + low)
-
-        def line(step_x, step_y):
+        for step in RING:
+            if step:
+                send(*route, ring[step] + low)
+            send(*route, ring[step] + twin)
+
+    def send_lines(*route, ready=None):
+        @pl.loop(1, 16)
+        def _(line):
+            step_x, step_y = line // 4, lax.rem(line, 4)
+            if ready is not None:
+                ready(lax.rem(4 - step_x, 4) * 4 + lax.rem(4 - step_y, 4))
             for step_core in range(2):
                 place = beside(step_x, step_y, step_core)
                 for step in RING:
-                    send(ring[step] + place)
-
-        for step in RING:
-            send(ring[step] + twin)
-        if wait_x is not None:
-            wait_x()
-
-        @pl.loop(1, 4)
-        def _(step_x):
-            line(step_x, 0)
-
-        for step_y in range(1, 4):
-            if wait_y is not None:
-                wait_y(step_y)
-
-            @pl.loop(0, 4)
-            def _(step_x):
-                line(step_x, step_y)
+                    send(*route, ring[step] + place)
 
     def all_in(incoming, part, in_sem):
         pltpu.make_async_copy(incoming.at[part], incoming.at[part], in_sem.at[part]).wait()
@@ -143,22 +135,17 @@
         pltpu.make_async_copy(span, span, out_sem.at[part]).wait()
 
     pack(0)
-    pl.semaphore_wait(barrier, 21)
-    for step in range(1, 4):
-        greet(cross_sem.at[0, step], ring[0] + beside(step, 0, 0))
-
-    def plane_in():
-        for step in range(1, 4):
-            pl.semaphore_wait(cross_sem.at[0, 4 - step], 1)
-        for step in range(1, 4):
-            greet(cross_sem.at[1, step], ring[0] + beside(0, step, 0))
-
-    def other_in(step):
-        pl.semaphore_wait(cross_sem.at[1, 4 - step], 1)
-
-    scatter(sent, landed, 0, send_sem, recv_sem, plane_in, other_in)
     pack(1)
-    scatter(sent, landed, 1, send_sem, recv_sem)
+    pl.semaphore_wait(barrier, 30)
+
+    @pl.loop(1, 16, unroll=5)
+    def _(line):
+        greet(cross_sem.at[line], ring[0] + beside(line // 4, lax.rem(line, 4), 0))
+
+    for part in range(PARTS):
+        send_own_line(sent, landed, part, send_sem, recv_sem)
+    send_lines(sent, landed, 0, send_sem, recv_sem, ready=lambda line: pl.semaphore_wait(cross_sem.at[line], 1))
+    send_lines(sent, landed, 1, send_sem, recv_sem)
 
     table_load.wait()
     split[0], split[1] = halves(table[pl.ds(0, 1536)])
@@ -206,7 +193,8 @@
         for line in range(LINES):
             result[pl.ds(line, DEVICES, stride=LINES), :] = final[:, line * TOKENS:(line + 1) * TOKENS]
         returned[part] = result[...].reshape(DEVICES, 3, HELD, TOKENS).astype(BF16)
-        scatter(returned, returned_in, part, return_sem, back_sem)
+        send_own_line(returned, returned_in, part, return_sem, back_sem)
+        send_lines(returned, returned_in, part, return_sem, back_sem)
 
     for part in range(PARTS):
         all_in(returned_in, part, back_sem)
@@ -262,7 +250,7 @@
             pltpu.SemaphoreType.DMA((PARTS,)),
             pltpu.SemaphoreType.DMA((PARTS,)),
             pltpu.SemaphoreType.DMA((PARTS,)),
-            pltpu.SemaphoreType.REGULAR((2, 4)),
+            pltpu.SemaphoreType.REGULAR((16,)),
         ],
         compiler_params=pltpu.CompilerParams(
             collective_id=0, has_side_effects=True, vmem_limit_bytes=40 * 2**20

time: 54.1 us -> 53.6 us (level)
  no operation moved by 1% of the time
where the time goes in v3:
time: 53.6 us; the launch traced here: 53.5 us
  Pallas kernels  52.8 us (99%)
  between operations  0.64 us (1%)
    pallas_call x1, Pallas kernels, on_device(): pl.pallas_call(kernel, out_shape=pltpu.VMEM((4,) + block, BF16), in_specs...  51.8 us

profile of v3, /device:TPU:1, one launch (start us, length us, event | category | flops | bytes accessed | tf_op | source)
XLA Modules:
  0.0 53.5 jit_solution(16185534693498084575)
XLA Ops:
  0.6 51.8 %transform_and_exchange.1.stacked = bf16[4,1024,128]{2,1,0:T(8,128)(2,1)S(1)} custom-call(bf16[1024,128]{1,0:T(8,128)(2,1)} %query_hbm.1, bf16[1024,128]{1,0:T(8,128)(2,1)} %key_hbm.1, bf16[1024,128]{1,0:T(8,128)(2,1)} %value_hbm.1, bf16[1024,128]{1,0:T(8,128)(2,1)} %taps_hbm.1, bf16[1024,128]{1,0:T(8,128)(2,1)} %grad_hbm.1, f32[1792,256]{1,0:T(8,128)} %constant.2.clone.table_hbm), custom_call_target="tpu_custom_call" | custom-call | tf_op jit(solution)/shard_map/transform_and_exchange/pallas_call | solution.py:233
  52.5 1.0 %gate_results.1 = (bf16[1024,128]{1,0:T(8,128)(2,1)}, bf16[1024,128]{1,0:T(8,128)(2,1)}, bf16[1024,128]{1,0:T(8,128)(2,1)}, bf16[1024,128]{1,0:T(8,128)(2,1)}) custom-call(bf16[4,1024,128]{2,1,0:T(8,128)(2,1)S(1)} %transform_and_exchange.1.stacked), custom_call_target="tpu_custom_call" | custom-call | tf_op jit(solution)/shard_map/gate_results/pallas_call | solution.py:260

commit v4 on v3

--- a/solution.py
+++ b/solution.py
@@ -60,21 +60,6 @@
     def beside(step_x, step_y, step_core):
         return lax.rem(column + step_x, 4) * 8 + lax.rem(row + step_y, 4) * 2 + lax.rem(core + step_core, 2)
 
-    barrier = pltpu.get_barrier_semaphore()
-
-    def greet(semaphore, device):
-        pl.semaphore_signal(semaphore, inc=1, device_id=device, device_id_type=LOGICAL)
-
-    twin = beside(0, 0, 1)
-    for step in RING:
-        if step:
-            greet(barrier, ring[step] + low)
-        greet(barrier, ring[step] + twin)
-
-    @pl.loop(1, 16, unroll=5)
-    def _(line):
-        greet(barrier, ring[0] + beside(line // 4, lax.rem(line, 4), 0))
-
     loads = []
     for part in range(PARTS):
         lines = pl.ds(part * SLAB, SLAB)
@@ -86,6 +71,21 @@
             copy.start()
             group.append(copy)
         loads.append(group)
+    barrier = pltpu.get_barrier_semaphore()
+
+    def greet(semaphore, device):
+        pl.semaphore_signal(semaphore, inc=1, device_id=device, device_id_type=LOGICAL)
+
+    twin = beside(0, 0, 1)
+    for step in RING:
+        if step:
+            greet(barrier, ring[step] + low)
+        greet(barrier, ring[step] + twin)
+
+    @pl.loop(1, 16, unroll=5)
+    def _(line):
+        greet(barrier, ring[0] + beside(line // 4, lax.rem(line, 4), 0))
+
     table_load = pltpu.make_async_copy(table_hbm, table, load_sem.at[0, 5])
     table_load.start()
 
@@ -156,7 +156,8 @@
 
     def triple(value, lines):
         high, below = halves(value)
-        return one_dot(high, split[0, lines]) + (one_dot(below, split[0, lines]) + one_dot(high, split[1, lines]))
+        tables = [split[0, lines], split[0, lines], split[1, lines]]
+        return one_dot(jnp.concatenate([high, below, high], axis=1), jnp.concatenate(tables, axis=0))
 
     @pl.loop(0, PARTS)
     def _(part):
@@ -165,7 +166,9 @@
         columns = jnp.concatenate(
             [rows[pl.ds(line, DEVICES, stride=LINES), :].astype(BF16) for line in range(LINES)], axis=1
         )
-        stage = one_dot(split[0, 0:512], columns) + one_dot(split[1, 0:512], columns)
+        stage = one_dot(
+            jnp.concatenate([split[0, 0:512], split[1, 0:512]], axis=1), jnp.concatenate([columns, columns], axis=0)
+        )
         freq = []
         for line in range(LINES):
             lanes = slice(line * TOKENS, (line + 1) * TOKENS)
@@ -185,11 +188,13 @@
                     imag = one[0] * two[1] - one[1] * two[0]
                 spread = triple(jnp.concatenate([real, imag], axis=1), slice(768, 1024))
                 pieces.append(twisted(spread[:, :TOKENS], spread[:, TOKENS:], -1.0))
-        final = 0.0
+        tables, values = [], []
         for side in range(2):
             high, below = halves(jnp.concatenate([piece[side] for piece in pieces], axis=1))
             lines = slice(1024 + side * DEVICES, 1280 + side * DEVICES)
-            final += one_dot(split[0, lines], high) + (one_dot(split[0, lines], below) + one_dot(split[1, lines], high))
+            tables += [split[0, lines], split[0, lines], split[1, lines]]
+            values += [high, below, high]
+        final = one_dot(jnp.concatenate(tables, axis=1), jnp.concatenate(values, axis=0))
         for line in range(LINES):
             result[pl.ds(line, DEVICES, stride=LINES), :] = final[:, line * TOKENS:(line + 1) * TOKENS]
         returned[part] = result[...].reshape(DEVICES, 3, HELD, TOKENS).astype(BF16)

time: 53.6 us -> 52.2 us (0.974)
  Pallas kernels: 52.8 us -> 51.5 us
    pallas_call x1, Pallas kernels: 51.8 us -> 50.5 us  [on_device(): pl.pallas_call(kernel, out_shape=pltpu.VMEM((4,) + block, BF16), in_specs...]
where the time goes in v4:
time: 52.2 us; the launch traced here: 52.1 us
  Pallas kernels  51.5 us (99%)
  between operations  0.64 us (1%)
    pallas_call x1, Pallas kernels, on_device(): pl.pallas_call(kernel, out_shape=pltpu.VMEM((4,) + block, BF16), in_specs...  50.5 us

profile of v4, /device:TPU:1, one launch (start us, length us, event | category | flops | bytes accessed | tf_op | source)
XLA Modules:
  0.0 52.1 jit_solution(4105622615297275391)
XLA Ops:
  0.6 50.5 %transform_and_exchange.1.stacked = bf16[4,1024,128]{2,1,0:T(8,128)(2,1)S(1)} custom-call(bf16[1024,128]{1,0:T(8,128)(2,1)} %query_hbm.1, bf16[1024,128]{1,0:T(8,128)(2,1)} %key_hbm.1, bf16[1024,128]{1,0:T(8,128)(2,1)} %value_hbm.1, bf16[1024,128]{1,0:T(8,128)(2,1)} %taps_hbm.1, bf16[1024,128]{1,0:T(8,128)(2,1)} %grad_hbm.1, f32[1792,256]{1,0:T(8,128)} %constant.2.clone.table_hbm), custom_call_target="tpu_custom_call" | custom-call | tf_op jit(solution)/shard_map/transform_and_exchange/pallas_call | solution.py:238
  51.1 1.0 %gate_results.1 = (bf16[1024,128]{1,0:T(8,128)(2,1)}, bf16[1024,128]{1,0:T(8,128)(2,1)}, bf16[1024,128]{1,0:T(8,128)(2,1)}, bf16[1024,128]{1,0:T(8,128)(2,1)}) custom-call(bf16[4,1024,128]{2,1,0:T(8,128)(2,1)S(1)} %transform_and_exchange.1.stacked), custom_call_target="tpu_custom_call" | custom-call | tf_op jit(solution)/shard_map/gate_results/pallas_call | solution.py:265

commit v5 on v4

--- a/solution.py
+++ b/solution.py
@@ -17,6 +17,11 @@
 ROWS = LINES * DEVICES
 SLAB = CHANNELS // PARTS
 RING = (4, 3, 5, 2, 6, 1, 7, 0)
+FAR, NEAR = RING[:5], RING[5:]
+TURNS = (2, 1, 3, 0)
+LINES_BY_HOPS = sorted(
+    ((x, y) for x in range(4) for y in range(4) if x or y), key=lambda line: -sum(min(step, 4 - step) for step in line)
+)
 BF16 = jnp.bfloat16
 F32 = jnp.float32
 
@@ -57,8 +62,10 @@
     core = lax.rem(low, 2)
     ring = [lax.rem(me // 32 + step, 8) * 32 for step in range(8)]
 
-    def beside(step_x, step_y, step_core):
-        return lax.rem(column + step_x, 4) * 8 + lax.rem(row + step_y, 4) * 2 + lax.rem(core + step_core, 2)
+    columns = [lax.rem(column + step, 4) * 8 for step in range(4)]
+    rows_of = [lax.rem(row + step, 4) * 2 for step in range(4)]
+    cores = [core, 1 - core]
+    twin = columns[0] + rows_of[0] + cores[1]
 
     loads = []
     for part in range(PARTS):
@@ -76,15 +83,18 @@
     def greet(semaphore, device):
         pl.semaphore_signal(semaphore, inc=1, device_id=device, device_id_type=LOGICAL)
 
-    twin = beside(0, 0, 1)
-    for step in RING:
+    def greet_lines(semaphore):
+        for x, y in LINES_BY_HOPS:
+            greet(semaphore(x * 4 + y), ring[0] + columns[x] + rows_of[y] + core)
+
+    for step in FAR:
+        greet(barrier, ring[step] + low)
+        greet(barrier, ring[step] + twin)
+    greet_lines(lambda line: barrier)
+    for step in NEAR:
         if step:
             greet(barrier, ring[step] + low)
         greet(barrier, ring[step] + twin)
-
-    @pl.loop(1, 16, unroll=5)
-    def _(line):
-        greet(barrier, ring[0] + beside(line // 4, lax.rem(line, 4), 0))
 
     table_load = pltpu.make_async_copy(table_hbm, table, load_sem.at[0, 5])
     table_load.start()
@@ -108,24 +118,56 @@
             device_id_type=LOGICAL,
         ).start()
 
+    def keep_own(outgoing, incoming, part, _, in_sem):
+        pltpu.make_async_copy(outgoing.at[part, me], incoming.at[part, me], in_sem.at[part]).start()
+
     def send_own_line(*route):
-        outgoing, incoming, part, _, in_sem = route
-        pltpu.make_async_copy(outgoing.at[part, me], incoming.at[part, me], in_sem.at[part]).start()
         for step in RING:
             if step:
                 send(*route, ring[step] + low)
             send(*route, ring[step] + twin)
 
-    def send_lines(*route, ready=None):
-        @pl.loop(1, 16)
-        def _(line):
-            step_x, step_y = line // 4, lax.rem(line, 4)
-            if ready is not None:
-                ready(lax.rem(4 - step_x, 4) * 4 + lax.rem(4 - step_y, 4))
-            for step_core in range(2):
-                place = beside(step_x, step_y, step_core)
-                for step in RING:
-                    send(*route, ring[step] + place)
+    def send_lines(*route, own):
+        for steps in (FAR, NEAR):
+
+            @pl.loop(0, 4)
+            def _(turn):
+                place_x = lax.rem(column + 2 + turn, 4) * 8
+                for y in TURNS:
+                    def line():
+                        for place_core in cores:
+                            for step in steps:
+                                if step or y or place_core is not core:
+                                    send(*route, ring[step] + place_x + rows_of[y] + place_core)
+                    if y or own:
+                        line()
+                    else:
+                        pl.when(turn != 2)(line)
+                if NEAR == steps:
+                    @pl.when(turn != 2)
+                    def _():
+                        send(*route, ring[0] + place_x + rows_of[0] + core)
+
+    my_plane = me // 32
+
+    def send_planes(*route, groups):
+        for planes in groups:
+
+            @pl.loop(0, 4)
+            def _(turn):
+                step_x = lax.rem(2 + turn, 4)
+                place_x = lax.rem(column + step_x, 4) * 8
+                for y in TURNS:
+                    for twin_step in range(2):
+                        place = place_x + rows_of[y] + cores[twin_step]
+                        for plane in planes:
+                            if y or twin_step:
+                                send(*route, plane * 32 + place)
+                            else:
+
+                                @pl.when(jnp.logical_or(step_x != 0, my_plane != plane))
+                                def _():
+                                    send(*route, plane * 32 + place)
 
     def all_in(incoming, part, in_sem):
         pltpu.make_async_copy(incoming.at[part], incoming.at[part], in_sem.at[part]).wait()
@@ -138,14 +180,21 @@
     pack(1)
     pl.semaphore_wait(barrier, 30)
 
-    @pl.loop(1, 16, unroll=5)
-    def _(line):
-        greet(cross_sem.at[line], ring[0] + beside(line // 4, lax.rem(line, 4), 0))
+    greet_lines(lambda line: cross_sem.at[line])
+
+    def send_when_ready(step_x, place_x, y):
+        pl.semaphore_wait(cross_sem.at[lax.rem(4 - step_x, 4) * 4 + (4 - y) % 4], 1)
+        for place_core in cores:
+            for step in RING:
+                send(sent, landed, 0, send_sem, recv_sem, ring[step] + place_x + rows_of[y] + place_core)
 
     for part in range(PARTS):
-        send_own_line(sent, landed, part, send_sem, recv_sem)
-    send_lines(sent, landed, 0, send_sem, recv_sem, ready=lambda line: pl.semaphore_wait(cross_sem.at[line], 1))
-    send_lines(sent, landed, 1, send_sem, recv_sem)
+        keep_own(sent, landed, part, send_sem, recv_sem)
+    send_own_line(sent, landed, 0, send_sem, recv_sem)
+    for x, y in [(0, 2), (1, 1), (1, 3), (2, 0), (3, 1), (3, 3), (1, 2), (2, 1), (2, 3), (3, 2), (2, 2), (0, 1), (0, 3), (1, 0), (3, 0)]:
+        send_when_ready(x, columns[x], y)
+    all_out(sent, 0, send_sem)
+    send_lines(sent, landed, 1, send_sem, recv_sem, own=True)
 
     table_load.wait()
     split[0], split[1] = halves(table[pl.ds(0, 1536)])
@@ -198,8 +247,14 @@
         for line in range(LINES):
             result[pl.ds(line, DEVICES, stride=LINES), :] = final[:, line * TOKENS:(line + 1) * TOKENS]
         returned[part] = result[...].reshape(DEVICES, 3, HELD, TOKENS).astype(BF16)
-        send_own_line(returned, returned_in, part, return_sem, back_sem)
-        send_lines(returned, returned_in, part, return_sem, back_sem)
+        keep_own(returned, returned_in, part, return_sem, back_sem)
+        @pl.when(part == 0)
+        def _():
+            send_planes(returned, returned_in, part, return_sem, back_sem, groups=((0, 1, 2, 3, 4, 5, 6, 7),))
+
+        @pl.when(part == 1)
+        def _():
+            send_planes(returned, returned_in, part, return_sem, back_sem, groups=((0,), (1,), (2,), (3,), (4, 6), (5, 7)))
 
     for part in range(PARTS):
         all_in(returned_in, part, back_sem)
@@ -211,8 +266,8 @@
         out[1, lines] = (back_signal * value[lines].astype(F32)).astype(BF16)
         out[2, lines] = (back_signal * key[lines].astype(F32)).astype(BF16)
         out[3, lines] = taps_grad.astype(BF16)
+    all_out(sent, 1, send_sem)
     for part in range(PARTS):
-        all_out(sent, part, send_sem)
         all_out(returned, part, return_sem)
 
 

time: 52.2 us -> 51.5 us (0.987)
  Pallas kernels: 51.5 us -> 50.6 us
    pallas_call x1, Pallas kernels: 50.5 us -> 49.6 us  [on_device(): pl.pallas_call(kernel, out_shape=pltpu.VMEM((4,) + block, BF16), in_specs...]
where the time goes in v5:
time: 51.5 us; the launch traced here: 51.3 us
  Pallas kernels  50.6 us (98%)
  between operations  0.64 us (1%)
    pallas_call x1, Pallas kernels, on_device(): pl.pallas_call(kernel, out_shape=pltpu.VMEM((4,) + block, BF16), in_specs...  49.6 us

profile of v5, /device:TPU:1, one launch (start us, length us, event | category | flops | bytes accessed | tf_op | source)
XLA Modules:
  0.0 51.3 jit_solution(8559568622566184808)
XLA Ops:
  0.6 49.6 %transform_and_exchange.1.stacked = bf16[4,1024,128]{2,1,0:T(8,128)(2,1)S(1)} custom-call(bf16[1024,128]{1,0:T(8,128)(2,1)} %query_hbm.1, bf16[1024,128]{1,0:T(8,128)(2,1)} %key_hbm.1, bf16[1024,128]{1,0:T(8,128)(2,1)} %value_hbm.1, bf16[1024,128]{1,0:T(8,128)(2,1)} %taps_hbm.1, bf16[1024,128]{1,0:T(8,128)(2,1)} %grad_hbm.1, f32[1792,256]{1,0:T(8,128)} %constant.2.clone.table_hbm), custom_call_target="tpu_custom_call" | custom-call | tf_op jit(solution)/shard_map/transform_and_exchange/pallas_call | solution.py:293
  50.3 1.0 %gate_results.1 = (bf16[1024,128]{1,0:T(8,128)(2,1)}, bf16[1024,128]{1,0:T(8,128)(2,1)}, bf16[1024,128]{1,0:T(8,128)(2,1)}, bf16[1024,128]{1,0:T(8,128)(2,1)}) custom-call(bf16[4,1024,128]{2,1,0:T(8,128)(2,1)S(1)} %transform_and_exchange.1.stacked), custom_call_target="tpu_custom_call" | custom-call | tf_op jit(solution)/shard_map/gate_results/pallas_call | solution.py:320

commit v6 on v5

--- a/solution.py
+++ b/solution.py
@@ -148,26 +148,19 @@
                     def _():
                         send(*route, ring[0] + place_x + rows_of[0] + core)
 
-    my_plane = me // 32
-
     def send_planes(*route, groups):
         for planes in groups:
 
             @pl.loop(0, 4)
-            def _(turn):
-                step_x = lax.rem(2 + turn, 4)
-                place_x = lax.rem(column + step_x, 4) * 8
-                for y in TURNS:
-                    for twin_step in range(2):
-                        place = place_x + rows_of[y] + cores[twin_step]
+            def _(place_x):
+                for y in range(4):
+                    for place_core in (1, 0):
                         for plane in planes:
-                            if y or twin_step:
-                                send(*route, plane * 32 + place)
-                            else:
-
-                                @pl.when(jnp.logical_or(step_x != 0, my_plane != plane))
-                                def _():
-                                    send(*route, plane * 32 + place)
+                            device = plane * 32 + place_x * 8 + y * 2 + place_core
+
+                            @pl.when(device != me)
+                            def _():
+                                send(*route, device)
 
     def all_in(incoming, part, in_sem):
         pltpu.make_async_copy(incoming.at[part], incoming.at[part], in_sem.at[part]).wait()
@@ -254,7 +247,7 @@
 
         @pl.when(part == 1)
         def _():
-            send_planes(returned, returned_in, part, return_sem, back_sem, groups=((0,), (1,), (2,), (3,), (4, 6), (5, 7)))
+            send_planes(returned, returned_in, part, return_sem, back_sem, groups=((0,), (1, 2), (3,), (4, 6), (5, 7)))
 
     for part in range(PARTS):
         all_in(returned_in, part, back_sem)

time: 51.5 us -> 50.3 us (0.977)
  the two profiles are of different devices: /device:TPU:1 before, /device:TPU:39 now
where the time goes in v6:
time: 50.3 us; the launch traced here: 50.2 us
  Pallas kernels  49.5 us (98%)
  between operations  0.64 us (1%)
    pallas_call x1, Pallas kernels, on_device(): pl.pallas_call(kernel, out_shape=pltpu.VMEM((4,) + block, BF16), in_specs...  48.5 us

profile of v6, /device:TPU:39, one launch (start us, length us, event | category | flops | bytes accessed | tf_op | source)
XLA Modules:
  0.0 50.2 jit_solution(15610308380721003186)
XLA Ops:
  0.6 48.5 %transform_and_exchange.1.stacked = bf16[4,1024,128]{2,1,0:T(8,128)(2,1)S(1)} custom-call(bf16[1024,128]{1,0:T(8,128)(2,1)} %query_hbm.1, bf16[1024,128]{1,0:T(8,128)(2,1)} %key_hbm.1, bf16[1024,128]{1,0:T(8,128)(2,1)} %value_hbm.1, bf16[1024,128]{1,0:T(8,128)(2,1)} %taps_hbm.1, bf16[1024,128]{1,0:T(8,128)(2,1)} %grad_hbm.1, f32[1792,256]{1,0:T(8,128)} %constant.2.clone.table_hbm), custom_call_target="tpu_custom_call" | custom-call | tf_op jit(solution)/shard_map/transform_and_exchange/pallas_call | solution.py:286
  49.2 1.0 %gate_results.1 = (bf16[1024,128]{1,0:T(8,128)(2,1)}, bf16[1024,128]{1,0:T(8,128)(2,1)}, bf16[1024,128]{1,0:T(8,128)(2,1)}, bf16[1024,128]{1,0:T(8,128)(2,1)}) custom-call(bf16[4,1024,128]{2,1,0:T(8,128)(2,1)S(1)} %transform_and_exchange.1.stacked), custom_call_target="tpu_custom_call" | custom-call | tf_op jit(solution)/shard_map/gate_results/pallas_call | solution.py:313

commit v7 on v6

--- a/solution.py
+++ b/solution.py
@@ -9,6 +9,7 @@
 LOGICAL = pl.DeviceIdType.LOGICAL
 DEVICES = 256
 INNER = 64
+HALF = DEVICES // 2
 TOKENS = 128
 CHANNELS = 1024
 PARTS = 2
@@ -113,13 +114,13 @@
             src_ref=outgoing.at[part, device],
             dst_ref=incoming.at[part, me],
             send_sem=out_sem.at[part],
-            recv_sem=in_sem.at[part],
+            recv_sem=in_sem,
             device_id=device,
             device_id_type=LOGICAL,
         ).start()
 
     def keep_own(outgoing, incoming, part, _, in_sem):
-        pltpu.make_async_copy(outgoing.at[part, me], incoming.at[part, me], in_sem.at[part]).start()
+        pltpu.make_async_copy(outgoing.at[part, me], incoming.at[part, me], in_sem).start()
 
     def send_own_line(*route):
         for step in RING:
@@ -162,8 +163,8 @@
                             def _():
                                 send(*route, device)
 
-    def all_in(incoming, part, in_sem):
-        pltpu.make_async_copy(incoming.at[part], incoming.at[part], in_sem.at[part]).wait()
+    def all_in(span, in_sem):
+        pltpu.make_async_copy(span, span, in_sem).wait()
 
     def all_out(outgoing, part, out_sem):
         span = outgoing.at[part, pl.ds(0, DEVICES - 1)]
@@ -179,15 +180,14 @@
         pl.semaphore_wait(cross_sem.at[lax.rem(4 - step_x, 4) * 4 + (4 - y) % 4], 1)
         for place_core in cores:
             for step in RING:
-                send(sent, landed, 0, send_sem, recv_sem, ring[step] + place_x + rows_of[y] + place_core)
+                send(sent, landed, 0, send_sem, recv_sem.at[0], ring[step] + place_x + rows_of[y] + place_core)
 
     for part in range(PARTS):
-        keep_own(sent, landed, part, send_sem, recv_sem)
-    send_own_line(sent, landed, 0, send_sem, recv_sem)
+        keep_own(sent, landed, part, send_sem, recv_sem.at[part])
+    send_own_line(sent, landed, 0, send_sem, recv_sem.at[0])
     for x, y in [(0, 2), (1, 1), (1, 3), (2, 0), (3, 1), (3, 3), (1, 2), (2, 1), (2, 3), (3, 2), (2, 2), (0, 1), (0, 3), (1, 0), (3, 0)]:
         send_when_ready(x, columns[x], y)
-    all_out(sent, 0, send_sem)
-    send_lines(sent, landed, 1, send_sem, recv_sem, own=True)
+    send_lines(sent, landed, 1, send_sem, recv_sem.at[1], own=True)
 
     table_load.wait()
     split[0], split[1] = halves(table[pl.ds(0, 1536)])
@@ -203,7 +203,7 @@
 
     @pl.loop(0, PARTS)
     def _(part):
-        all_in(landed, part, recv_sem)
+        all_in(landed.at[part], recv_sem.at[part])
         rows[...] = landed[part].astype(F32).reshape(ROWS, TOKENS)
         columns = jnp.concatenate(
             [rows[pl.ds(line, DEVICES, stride=LINES), :].astype(BF16) for line in range(LINES)], axis=1
@@ -240,27 +240,29 @@
         for line in range(LINES):
             result[pl.ds(line, DEVICES, stride=LINES), :] = final[:, line * TOKENS:(line + 1) * TOKENS]
         returned[part] = result[...].reshape(DEVICES, 3, HELD, TOKENS).astype(BF16)
-        keep_own(returned, returned_in, part, return_sem, back_sem)
+        keep_own(returned, returned_in, part, return_sem, back_sem.at[part, me // HALF])
         @pl.when(part == 0)
         def _():
-            send_planes(returned, returned_in, part, return_sem, back_sem, groups=((0, 1, 2, 3, 4, 5, 6, 7),))
+            send_planes(returned, returned_in, part, return_sem, back_sem.at[part, me // HALF], groups=((0, 2, 4, 6), (1, 3, 5, 7)))
 
         @pl.when(part == 1)
         def _():
-            send_planes(returned, returned_in, part, return_sem, back_sem, groups=((0,), (1, 2), (3,), (4, 6), (5, 7)))
+            send_planes(returned, returned_in, part, return_sem, back_sem.at[part, me // HALF], groups=((0,), (1, 2), (3, 4, 7), (5, 6)))
 
     for part in range(PARTS):
-        all_in(returned_in, part, back_sem)
-        lines = pl.ds(part * SLAB, SLAB)
-        convolved, back_signal, taps_grad = (
-            returned_in[part, :, which].astype(F32).reshape(SLAB, TOKENS) for which in range(3)
-        )
-        out[0, lines] = (grad[lines].astype(F32) * convolved).astype(BF16)
-        out[1, lines] = (back_signal * value[lines].astype(F32)).astype(BF16)
-        out[2, lines] = (back_signal * key[lines].astype(F32)).astype(BF16)
-        out[3, lines] = taps_grad.astype(BF16)
-    all_out(sent, 1, send_sem)
+        for half in range(2):
+            all_in(returned_in.at[part, pl.ds(half * HALF, HALF)], back_sem.at[part, half])
+            lines = pl.ds(part * SLAB + half * (SLAB // 2), SLAB // 2)
+            convolved, back_signal, taps_grad = (
+                returned_in[part, pl.ds(half * HALF, HALF), which].astype(F32).reshape(SLAB // 2, TOKENS)
+                for which in range(3)
+            )
+            out[0, lines] = (grad[lines].astype(F32) * convolved).astype(BF16)
+            out[1, lines] = (back_signal * value[lines].astype(F32)).astype(BF16)
+            out[2, lines] = (back_signal * key[lines].astype(F32)).astype(BF16)
+            out[3, lines] = taps_grad.astype(BF16)
     for part in range(PARTS):
+        all_out(sent, part, send_sem)
         all_out(returned, part, return_sem)
 
 
@@ -302,7 +304,7 @@
             pltpu.SemaphoreType.DMA((PARTS,)),
             pltpu.SemaphoreType.DMA((PARTS,)),
             pltpu.SemaphoreType.DMA((PARTS,)),
-            pltpu.SemaphoreType.DMA((PARTS,)),
+            pltpu.SemaphoreType.DMA((PARTS, 2)),
             pltpu.SemaphoreType.REGULAR((16,)),
         ],
         compiler_params=pltpu.CompilerParams(

time: 50.3 us -> 50 us (level)
  no operation moved by 1% of the time
where the time goes in v7:
time: 50 us; the launch traced here: 49.9 us
  Pallas kernels  49.2 us (98%)
  between operations  0.64 us (1%)
    pallas_call x1, Pallas kernels, on_device(): pl.pallas_call(kernel, out_shape=pltpu.VMEM((4,) + block, BF16), in_specs...  48.2 us

profile of v7, /device:TPU:39, one launch (start us, length us, event | category | flops | bytes accessed | tf_op | source)
XLA Modules:
  0.0 49.9 jit_solution(6802779789448818820)
XLA Ops:
  0.6 48.2 %transform_and_exchange.1.stacked = bf16[4,1024,128]{2,1,0:T(8,128)(2,1)S(1)} custom-call(bf16[1024,128]{1,0:T(8,128)(2,1)} %query_hbm.1, bf16[1024,128]{1,0:T(8,128)(2,1)} %key_hbm.1, bf16[1024,128]{1,0:T(8,128)(2,1)} %value_hbm.1, bf16[1024,128]{1,0:T(8,128)(2,1)} %taps_hbm.1, bf16[1024,128]{1,0:T(8,128)(2,1)} %grad_hbm.1, f32[1792,256]{1,0:T(8,128)} %constant.2.clone.table_hbm), custom_call_target="tpu_custom_call" | custom-call | tf_op jit(solution)/shard_map/transform_and_exchange/pallas_call | solution.py:288
  48.9 1.0 %gate_results.1 = (bf16[1024,128]{1,0:T(8,128)(2,1)}, bf16[1024,128]{1,0:T(8,128)(2,1)}, bf16[1024,128]{1,0:T(8,128)(2,1)}, bf16[1024,128]{1,0:T(8,128)(2,1)}) custom-call(bf16[4,1024,128]{2,1,0:T(8,128)(2,1)S(1)} %transform_and_exchange.1.stacked), custom_call_target="tpu_custom_call" | custom-call | tf_op jit(solution)/shard_map/gate_results/pallas_call | solution.py:315
